TPU v7x, 32 devices: a whole 2x2x4 slice. The times are simulated.
32 devices in a mesh: gx: 4 (over z), gy: 8 (over y, x, core).
Axes of the slice: x: 2, y: 2, z: 4, core: 2. Of those that a mesh axis runs over, the one named last changes fastest.
Arguments:
- observed: float32 [2, 8192, 8192], P(None, 'gx', 'gy'), may hold values from -6 to 6
- noise_var: float32 [8192, 8192], P('gx', 'gy'), may hold values from 0.05 to 0.5
- row_kernel: float32 [4096, 4096], P('gx'), may hold values from -1 to 1.2, as said below
- col_kernel: float32 [4096, 4096], P('gy'), may hold values from -1 to 1.2, as said below
Outputs:
- gram_times: float32 [2, 8192, 8192], P(None, 'gx', 'gy')
Inputs may be any that keep to these rules, and one draw needn't show every extreme that they name: row_kernel is symmetric. col_kernel is symmetric.
All inputs are finite; a program needn't handle non-finite values.
Results may differ from a plain program's by a relative error of at most 0.000065.
Values sent between devices are 32-bit elements; how exact they have to be, the bound alone decides.
A program may use at most 192 MiB of HBM per device.

v0:
```python
import jax
import jax.numpy as jnp
from jax import lax
from jax.sharding import PartitionSpec as P

even_taps = (-0.0703125, 0.8671875, 0.2265625, -0.0234375)
odd_taps = (-0.0234375, 0.2265625, 0.8671875, -0.0703125)


def with_halo(cells, sides, width):
    for axis, dim in sides:
        count = lax.axis_size(axis)
        ends = count - 1
        head = lax.slice_in_dim(cells, 0, width, axis=dim)
        tail = lax.slice_in_dim(cells, cells.shape[dim] - width, cells.shape[dim], axis=dim)
        cells = jnp.concatenate(
            [
                lax.ppermute(tail, axis, [(i, (i + 1) % count) for i in range(ends)]),
                cells,
                lax.ppermute(head, axis, [((i + 1) % count, i) for i in range(ends)]),
            ],
            axis=dim,
        )
    return cells


def keys_weight(dist):
    span = jnp.abs(dist)
    inner = (1.5 * span - 2.5) * span * span + 1.0
    outer = ((-0.5 * span + 2.5) * span - 4.0) * span + 2.0
    return jnp.where(span < 1.0, inner, jnp.where(span < 2.0, outer, 0.0))


def adjoint_rows(extended, count):
    evens = extended[:, 0::2]
    odds = extended[:, 1::2]
    total = jnp.zeros((extended.shape[0], count, extended.shape[2]), jnp.float32)
    for index in range(4):
        start = 3 - index
        total = (
            total
            + even_taps[index] * evens[:, start : start + count]
            + odd_taps[index] * odds[:, start : start + count]
        )
    return total


def forward_rows(extended, count):
    first = jnp.zeros((extended.shape[0], count, extended.shape[2]), jnp.float32)
    second = jnp.zeros((extended.shape[0], count, extended.shape[2]), jnp.float32)
    for index in range(4):
        start = index + 1
        first = first + even_taps[index] * extended[:, start : start + count]
        second = second + odd_taps[index] * extended[:, start : start + count]
    stacked = jnp.stack([first, second], axis=2)
    return stacked.reshape(extended.shape[0], 2 * count, extended.shape[2])


def body(observed, noise_var, row_kernel, col_kernel):
    highest = lax.Precision.HIGHEST
    tile_rows = row_kernel.shape[0]
    tile_cols = col_kernel.shape[0]
    extended = with_halo(observed, (("gx", 1), ("gy", 2)), 4)
    rowsum = adjoint_rows(extended, tile_rows)
    fine_index = lax.broadcasted_iota(jnp.float32, (2 * tile_cols + 8, tile_cols), 0)
    coarse_index = lax.broadcasted_iota(jnp.float32, (2 * tile_cols + 8, tile_cols), 1)
    adjoint_table = keys_weight(coarse_index - ((fine_index - 4.0) * 0.5 + 0.25))
    inducing = jnp.einsum("riq,qj->rij", rowsum, adjoint_table, precision=highest)
    block = col_kernel
    mixed = jnp.einsum(
        "rik,jk->rij", lax.all_gather(inducing, "gy", axis=2, tiled=True), block, precision=highest
    )
    block = row_kernel
    product = jnp.einsum(
        "ik,rkj->rij", block, lax.all_gather(mixed, "gx", axis=1, tiled=True), precision=highest
    )
    coarse_ext = with_halo(product, (("gx", 1), ("gy", 2)), 2)
    coarse_pos = lax.broadcasted_iota(jnp.float32, (tile_cols + 4, 2 * tile_cols), 0)
    fine_pos = lax.broadcasted_iota(jnp.float32, (tile_cols + 4, 2 * tile_cols), 1)
    forward_table = keys_weight(coarse_pos - 2.0 - (fine_pos * 0.5 + 0.25))
    colpass = jnp.einsum("riq,qp->rip", coarse_ext, forward_table, precision=highest)
    result = forward_rows(colpass, tile_rows)
    return result + noise_var[None] * observed


def solution(mesh):
    return jax.shard_map(
        body,
        mesh=mesh,
        in_specs=(P(None, "gx", "gy"), P("gx", "gy"), P("gx", None), P("gy", None)),
        out_specs=P(None, "gx", "gy"),
        check_vma=False,
    )
```

profile of v0, /device:TPU:0, one launch (start us, length us, event | category | flops | bytes accessed | tf_op | source)
XLA Modules:
  0.0 1504.2 jit_solution(3268729473362996440)
XLA Ops:
  6.5 0.9 fusion.107
  7.4 4.9 collective-permute-start
  12.4 1.3 collective-permute-start.1
  13.7 17.3 %copy.23 = f32[2,2048,1024]{1,2,0:T(8,128)} copy(f32[2,2048,1024]{2,1,0:T(8,128)} %param.4) | data formatting | bytes 33554432 | tf_op args[0]
  31.7 21.6 %concatenate.12 = f32[2,2056,1024]{1,2,0:T(8,128)} concatenate(f32[2,4,1024]{1,2,0:T(8,128)S(1)} %copy.22, f32[2,2048,1024]{1,2,0:T(8,128)} %copy.23, f32[2,4,1024]{1,2,0:T(8,128)S(1)} %copy.24), dimensions={1} | concatenate | bytes 33685504 | tf_op jit(solution)/shard_map/concatenate | solution.py:16
  53.4 1.0 fusion.106
  54.4 1.5 collective-permute-start.2
  55.9 1.3 collective-permute-start.3
  57.2 3.4 collective-permute-done.3
  60.6 51.5 %concatenate.13 = f32[2,2056,1032]{1,2,0:T(8,128)} concatenate(f32[2,2056,4]{1,2,0:T(4,128)S(1)} %collective-permute-done.2, f32[2,2056,1024]{1,2,0:T(8,128)} %concatenate.12, f32[2,2056,4]{1,2,0:T(4,128)S(1)} %collective-permute-done.3), dimensions={2} | concatenate | bytes 33948672 | tf_op jit(solution)/shard_map/concatenate | solution.py:16
  112.1 290.8 %slice.74 = f32[2,1028,1032]{1,2,0:T(8,128)} slice(f32[2,2056,1032]{1,2,0:T(8,128)} %concatenate.13), slice={[0:2:1], [0:2056:2], [0:1032:1]} | slice | bytes 16974336 | tf_op jit(solution)/shard_map/slice | solution.py:35
  402.9 290.8 %slice.76 = f32[2,1028,1032]{1,2,0:T(8,128)} slice(f32[2,2056,1032]{1,2,0:T(8,128)} %concatenate.13), slice={[0:2:1], [1:2056:2], [0:1032:1]} | slice | bytes 16974336 | tf_op jit(solution)/shard_map/slice | solution.py:36
  693.7 42.8 %fusion.3 = f32[2,1024,512]{2,1,0:T(8,128)} fusion(f32[2,1028,1032]{1,2,0:T(8,128)} %slice.76, f32[2,1028,1032]{1,2,0:T(8,128)} %slice.74, f32[1032]{0:T(1024)S(1)} %multiply_add_fusion), kind=kOutput, calls=%fused_computation.6 | convolution fusion | flops 13026250752 | bytes 71831584 | tf_op jit(solution)/shard_map/riq,qj->rij/dot_general | solution.py:68
  736.5 165.8 %all-gather.3.cloned.1.call-done = f32[2,1024,4096]{2,1,0:T(8,128)} async-done(((f32[2,1024,512]{2,1,0:T(8,128)}), f32[2,1024,4096]{2,1,0:T(8,128)}) %all-gather.3.cloned.1.call-update) | async-done | bytes 33554448 | tf_op jit(solution)/shard_map/all_gather | solution.py:71
  902.3 60.3 %fusion.17 = f32[2,1024,512]{2,1,0:T(8,128)} fusion(f32[2,1024,4096]{2,1,0:T(8,128)} %all-gather.3.cloned.1.call-done, f32[512,4096]{1,0:T(8,128)} %param.7), kind=kOutput, calls=%fused_computation.20 | convolution fusion | flops 51539607552 | bytes 46137344 | tf_op jit(solution)/shard_map/rik,jk->rij/dot_general | solution.py:70
  962.6 286.9 %all-gather.5.cloned.1.call-done = f32[2,4096,512]{2,1,0:T(8,128)} async-done(((f32[2,1024,512]{2,1,0:T(8,128)}), f32[2,4096,512]{2,1,0:T(8,128)}) %all-gather.5.cloned.1.call-update) | async-done | bytes 16777232 | tf_op jit(solution)/shard_map/all_gather | solution.py:75
  1249.5 108.4 %fusion.29 = f32[2,1024,512]{1,2,0:T(8,128)S(1)} fusion(f32[2,4096,512]{2,1,0:T(8,128)} %all-gather.5.cloned.1.call-done, f32[1024,4096]{1,0:T(8,128)} %param.6), kind=kOutput, calls=%fused_computation.36 | convolution fusion | flops 51539607552 | bytes 37748736 | tf_op jit(solution)/shard_map/ik,rkj->rij/dot_general | solution.py:74
  1358.0 2.0 copy-done
  1360.2 1.3 collective-permute-start.4
  1361.6 1.3 collective-permute-start.5
  1362.9 10.3 collective-permute-done.4
  1373.2 4.1 collective-permute-done.5
  1377.3 6.4 concatenate.14
  1383.7 0.9 fusion.108
  1384.6 1.3 collective-permute-start.6
  1385.9 1.3 collective-permute-start.7
  1387.3 3.5 collective-permute-done.7
  1390.7 26.4 %fusion.19 = f32[2,1028,1024]{2,1,0:T(8,128)} fusion(f32[2,1028,2]{1,2,0:T(2,128)S(1)} %collective-permute-done.7, f32[2,1028,512]{1,2,0:T(8,128)} %concatenate.14, f32[2,1028,2]{1,2,0:T(2,128)S(1)} %collective-permute-done.6, f32[1024]{0:T(1024)S(1)} %multiply_add_fusion.1, f32[516]{0:T(1024)S(1)} %iota_add_fusion), kind=kOutput, calls=%fused_computation.24 | convolution fusion | flops 13047394304 | bytes 12671120 | tf_op jit(solution)/shard_map/riq,qp->rip/dot_general | solution.py:81
  1417.1 20.9 %add_bitcast_fusion.1 = (f32[2,1024,1,1024]{3,1,0,2:T(8,128)}, f32[2,1024,1,1024]{3,1,0,2:T(8,128)}) fusion(f32[2,1028,1024]{2,1,0:T(8,128)} %fusion.19), kind=kLoop, calls=%fused_computation.23 | loop fusion | flops 29360128 | bytes 50331648 | tf_op jit(solution)/shard_map/stack | solution.py:55
  1438.0 13.0 pad_maximum_fusion
  1451.0 28.7 %copy.26 = f32[2,1024,2,1024]{3,0,2,1:T(2,128)} copy(f32[2,1024,2,1024]{3,1,0,2:T(8,128)} %pad_maximum_fusion) | data formatting | bytes 33554432 | tf_op jit(solution)/shard_map/stack | solution.py:55
  1479.8 17.3 %copy_add_fusion = f32[2,2048,1024]{2,1,0:T(8,128)} fusion(f32[2,2048,1024]{2,0,1:T(2,128)} %bitcast.25, f32[2,2048,1024]{2,1,0:T(8,128)S(1)} %bitcast.24, f32[2048,1024]{1,0:T(8,128)} %param.5), kind=kLoop, calls=%fused_computation.3 | loop fusion | flops 8388608 | bytes 58720256 | tf_op jit(solution)/shard_map/add | solution.py:83
  (24 shorter events, 1.1 us)
Async XLA Ops:
  6.5 895.8 %all-gather.3.cloned.1.call-start = ((), (), s32[]{:S(2)}) async-start(), calls=%async_computation | async-start | bytes 37748736 | tf_op jit(solution)/shard_map/all_gather | solution.py:71
  7.4 23.6 %collective-permute-start = (f32[2,4,1024]{2,1,0:T(4,128)S(1)}, f32[2,4,1024]{2,1,0:T(4,128)S(1)}, u32[]{:S(2)}, u32[]{:S(2)}) collective-permute-start(f32[2,4,1024]{2,1,0:T(4,128)S(1)} %get-tuple-element.8), channel_id=1, source_target_pairs={{0,8},{8,16},{16,24},{1,9},{9,17},{17,25},{2,10},{10,18},{18,26},{... | collective-permute-start | bytes 98312 | tf_op jit(solution)/shard_map/ppermute | solution.py:18
  12.4 19.0 %collective-permute-start.1 = (f32[2,4,1024]{2,1,0:T(4,128)S(1)}, f32[2,4,1024]{2,1,0:T(4,128)S(1)}, u32[]{:S(2)}, u32[]{:S(2)}) collective-permute-start(f32[2,4,1024]{2,1,0:T(4,128)S(1)} %get-tuple-element.7), channel_id=1, source_target_pairs={{8,0},{16,8},{24,16},{9,1},{17,9},{25,17},{10,2},{18,10},{26,18},{... | collective-permute-start | bytes 98312 | tf_op jit(solution)/shard_map/ppermute | solution.py:20
  54.4 2.8 collective-permute-start.2
  55.9 4.7 collective-permute-start.3
  736.5 513.1 %all-gather.5.cloned.1.call-start = ((), (), s32[]{:S(2)}) async-start(), calls=%async_computation.1 | async-start | bytes 20971520 | tf_op jit(solution)/shard_map/all_gather | solution.py:75
  1358.0 2.0 copy-start
  1360.2 13.0 collective-permute-start.4
  1361.6 15.8 %collective-permute-start.5 = (f32[2,2,512]{1,2,0:T(8,128)S(1)}, f32[2,2,512]{1,2,0:T(8,128)S(1)}, u32[]{:S(2)}, u32[]{:S(2)}) collective-permute-start(f32[2,2,512]{1,2,0:T(8,128)S(1)} %get-tuple-element.13), channel_id=1, source_target_pairs={{8,0},{16,8},{24,16},{9,1},{17,9},{25,17},{10,2},{18,10},{26,18},{... | collective-permute-start | bytes 24584 | tf_op jit(solution)/shard_map/ppermute | solution.py:20
  1384.6 2.6 collective-permute-start.6
  1385.9 4.8 collective-permute-start.7
  1438.0 41.8 %slice-start = ((s8[16777216]{0:T(1024)(128)(4,1)}), s8[4194304]{0:T(1024)(128)(4,1)S(1)}, s32[]{:S(2)}) async-start(s8[16777216]{0:T(1024)(128)(4,1)} %bitcast.23), calls=%async_computation.2 | async-start | bytes 8388608
  1438.0 41.8 %slice-start.1 = ((s8[16777216]{0:T(1024)(128)(4,1)}), s8[4194304]{0:T(1024)(128)(4,1)S(1)}, s32[]{:S(2)}) async-start(s8[16777216]{0:T(1024)(128)(4,1)} %bitcast.23), calls=%async_computation.3 | async-start | bytes 8388608
  1451.0 28.8 %slice-start.2 = ((s8[16777216]{0:T(1024)(128)(4,1)}), s8[4194304]{0:T(1024)(128)(4,1)S(1)}, s32[]{:S(2)}) async-start(s8[16777216]{0:T(1024)(128)(4,1)} %bitcast.23), calls=%async_computation.4 | async-start | bytes 8388608
  1451.0 28.8 %slice-start.3 = ((s8[16777216]{0:T(1024)(128)(4,1)}), s8[4194304]{0:T(1024)(128)(4,1)S(1)}, s32[]{:S(2)}) async-start(s8[16777216]{0:T(1024)(128)(4,1)} %bitcast.23), calls=%async_computation.5 | async-start | bytes 8388608
Sparse Core Ops, SparseCore 0:
  736.6 165.6 all-gather.2
  962.7 286.7 all-gather.4
where the time goes:
time: 1520 us; the launch traced here: 1500 us
  local copies, waits for them, and re-layouts  713 us (47%)
  waiting for transfers between devices  474 us (31%)
  matrix products  238 us (16%)
  other arithmetic  51.2 us (3%)
    slice x1, local copies, waits for them, and re-layouts, adjoint_rows(): odds = extended[:, 1::2]  291 us
    slice x1, local copies, waits for them, and re-layouts, adjoint_rows(): evens = extended[:, 0::2]  291 us
    all_gather x1, waiting for transfers between devices, body(): lax.all_gather(mixed, 'gx', axis=1, tiled=True)  287 us
    all_gather x1, waiting for transfers between devices, body(): lax.all_gather(inducing, 'gy', axis=2, tiled=True)  166 us
    dot_general x1, matrix products, body(): jnp.einsum('ik,rkj->rij', block, lax.all_gather(mixed, 'gx', axis=1, tile...  108 us
    concatenate x3, local copies, waits for them, and re-layouts, with_halo(): jnp.concatenate([lax.ppermute(tail, axis, [(i, (i + 1) % count) for i in...  79.5 us
    dot_general x1, matrix products, body(): jnp.einsum('rik,jk->rij', lax.all_gather(inducing, 'gy', axis=2, tiled=Tr...  60.3 us
    dot_general x1, matrix products, body(): jnp.einsum('riq,qj->rij', rowsum, adjoint_table, precision=highest)  42.8 us
  transfers between devices with their start and end apart: 10, of which 6 were waited for; matrix products, arithmetic and copies ran while one was open for 1% of the time, Pallas kernels for 0%

commit v1 on v0

v1 whole, which is shorter than its diff:
```python
import jax
import jax.numpy as jnp
from jax import lax
from jax.experimental import pallas as pl
from jax.experimental.pallas import tpu as pltpu
from jax.sharding import PartitionSpec as P

PAD = 8
BAND = 256
VMEM_BYTES = 48 * 1024 * 1024


def keys_weight(dist):
    span = jnp.abs(dist)
    inner = (1.5 * span - 2.5) * span * span + 1.0
    outer = ((-0.5 * span + 2.5) * span - 4.0) * span + 2.0
    return jnp.where(span < 1.0, inner, jnp.where(span < 2.0, outer, 0.0))


def weights(coarse, fine):
    return keys_weight(coarse - (fine * 0.5 + 0.25)).astype(jnp.bfloat16)


def positions(size, offset):
    return jnp.arange(size, dtype=jnp.float32) + offset


def halo_positions(width, cols):
    lane = jnp.arange(128)
    place = jnp.where(lane < width, lane - width, cols + lane - width)
    far = jnp.where(lane < 2 * width, place, -1000000)
    return far.astype(jnp.float32)


def neighbours(cells, axis, dim, width):
    count = lax.axis_size(axis)
    head = lax.slice_in_dim(cells, 0, width, axis=dim)
    tail = lax.slice_in_dim(cells, cells.shape[dim] - width, cells.shape[dim], axis=dim)
    before = lax.ppermute(tail, axis, [(i, i + 1) for i in range(count - 1)])
    after = lax.ppermute(head, axis, [(i + 1, i) for i in range(count - 1)])
    return before, after


def side_strips(cells, above, below, width):
    strip_first = jnp.concatenate([part[..., :width] for part in (above, cells, below)], axis=1)
    strip_last = jnp.concatenate([part[..., -width:] for part in (above, cells, below)], axis=1)
    count = lax.axis_size("gy")
    left = lax.ppermute(strip_last, "gy", [(i, i + 1) for i in range(count - 1)])
    right = lax.ppermute(strip_first, "gy", [(i + 1, i) for i in range(count - 1)])
    both = jnp.concatenate([left, right], axis=2)
    return jnp.pad(both, ((0, 0), (0, 0), (0, 128 - 2 * width)))


def split(value):
    high = value.astype(jnp.bfloat16)
    return high, (value - high.astype(jnp.float32)).astype(jnp.bfloat16)


def exact_left(table, value):
    high, low = split(value)
    return jnp.dot(table, high, preferred_element_type=jnp.float32) + jnp.dot(
        table, low, preferred_element_type=jnp.float32
    )


def exact_right(value, table):
    high, low = split(value)
    return jnp.dot(high, table, preferred_element_type=jnp.float32) + jnp.dot(
        low, table, preferred_element_type=jnp.float32
    )


def extended_rows(main, before, after, above, below):
    step = pl.program_id(1)
    first = jnp.where(step == 0, above[0], before[0])
    last = jnp.where(step == pl.num_programs(1) - 1, below[0], after[0])
    return jnp.concatenate([first, main[0], last], axis=0)


def adjoint_kernel(main, before, after, above, below, sides, row_table, col_table, side_table, out):
    step = pl.program_id(1)
    cells = extended_rows(main, before, after, above, below)
    rows = exact_left(row_table[...], cells)
    start = pl.multiple_of(step * 2 * BAND, 2 * BAND)
    edge = exact_left(row_table[...], sides[0, pl.ds(start, 2 * BAND + 2 * PAD), :])
    out[0] = exact_right(rows, col_table[...]) + exact_right(edge, side_table[...])


def forward_kernel(
    main, before, after, above, below, sides, row_table, col_table, side_table, noise, observed, out
):
    step = pl.program_id(1)
    cells = extended_rows(main, before, after, above, below)
    start = pl.multiple_of(step * BAND, BAND)
    edge = sides[0, pl.ds(start, BAND + 2 * PAD), :]
    cols = exact_right(cells, col_table[...]) + exact_right(edge, side_table[...])
    out[0] = exact_left(row_table[...], cols) + noise[...] * observed[0]


def banded_specs(rows, cols, band):
    per = band // PAD
    last = rows // PAD - 1
    return [
        pl.BlockSpec((1, band, cols), lambda r, i: (r, i, 0)),
        pl.BlockSpec((1, PAD, cols), lambda r, i: (r, jnp.maximum(i * per - 1, 0), 0)),
        pl.BlockSpec((1, PAD, cols), lambda r, i: (r, jnp.minimum((i + 1) * per, last), 0)),
        pl.BlockSpec((1, PAD, cols), lambda r, i: (r, 0, 0)),
        pl.BlockSpec((1, PAD, cols), lambda r, i: (r, 0, 0)),
        pl.BlockSpec((1, rows + 2 * PAD, 128), lambda r, i: (r, 0, 0)),
    ]


def whole(table):
    return pl.BlockSpec(table.shape, lambda r, i: (0, 0))


def adjoint(observed):
    rhs, rows, cols = observed.shape
    above, below = neighbours(observed, "gx", 1, PAD)
    sides = side_strips(observed, above, below, 4)
    coarse = cols // 2
    row_table = weights(positions(BAND, 0)[:, None], positions(2 * BAND + 2 * PAD, -PAD)[None, :])
    col_table = weights(positions(coarse, 0)[None, :], positions(cols, 0)[:, None])
    side_table = weights(positions(coarse, 0)[None, :], halo_positions(4, cols)[:, None])
    return pl.pallas_call(
        adjoint_kernel,
        grid=(rhs, rows // (2 * BAND)),
        in_specs=banded_specs(rows, cols, 2 * BAND)
        + [whole(row_table), whole(col_table), whole(side_table)],
        out_specs=pl.BlockSpec((1, BAND, coarse), lambda r, i: (r, i, 0)),
        out_shape=jax.ShapeDtypeStruct((rhs, rows // 2, coarse), jnp.float32),
        compiler_params=pltpu.CompilerParams(vmem_limit_bytes=VMEM_BYTES),
    )(observed, observed, observed, above, below, sides, row_table, col_table, side_table)


def forward(product, noise_var, observed):
    rhs, rows, cols = product.shape
    above, below = neighbours(product, "gx", 1, PAD)
    sides = side_strips(product, above, below, 2)
    fine = 2 * cols
    row_table = weights(positions(BAND + 2 * PAD, -PAD)[None, :], positions(2 * BAND, 0)[:, None])
    col_table = weights(positions(cols, 0)[:, None], positions(fine, 0)[None, :])
    side_table = weights(halo_positions(2, cols)[:, None], positions(fine, 0)[None, :])
    return pl.pallas_call(
        forward_kernel,
        grid=(rhs, rows // BAND),
        in_specs=banded_specs(rows, cols, BAND)
        + [
            whole(row_table),
            whole(col_table),
            whole(side_table),
            pl.BlockSpec((2 * BAND, fine), lambda r, i: (i, 0)),
            pl.BlockSpec((1, 2 * BAND, fine), lambda r, i: (r, i, 0)),
        ],
        out_specs=pl.BlockSpec((1, 2 * BAND, fine), lambda r, i: (r, i, 0)),
        out_shape=jax.ShapeDtypeStruct((rhs, 2 * rows, fine), jnp.float32),
        compiler_params=pltpu.CompilerParams(vmem_limit_bytes=VMEM_BYTES),
    )(
        product, product, product, above, below, sides,
        row_table, col_table, side_table, noise_var, observed,
    )


def by_columns(field, col_kernel):
    gathered = lax.all_gather(field, "gy", axis=1, tiled=True)
    return jnp.einsum("ik,jk->ij", gathered, col_kernel, precision=lax.Precision.HIGH)


def by_rows(field, row_kernel):
    gathered = lax.all_gather(field, "gx", axis=0, tiled=True)
    return jnp.einsum("ik,kj->ij", row_kernel, gathered, precision=lax.Precision.HIGH)


def body(observed, noise_var, row_kernel, col_kernel):
    inducing = adjoint(observed)
    one = by_rows(by_columns(inducing[0], col_kernel), row_kernel)
    two = by_columns(by_rows(inducing[1], row_kernel), col_kernel)
    return forward(jnp.stack([one, two]), noise_var, observed)


def solution(mesh):
    return jax.shard_map(
        body,
        mesh=mesh,
        in_specs=(P(None, "gx", "gy"), P("gx", "gy"), P("gx", None), P("gy", None)),
        out_specs=P(None, "gx", "gy"),
        check_vma=False,
    )
```

time: 1520 us -> 630 us (0.41)
  local copies, waits for them, and re-layouts: 713 us -> 22.3 us
  matrix products: 238 us -> 103 us
  waiting for transfers between devices: 474 us -> 410 us
  Pallas kernels: 0 us -> 42.9 us
  other arithmetic: 51.2 us -> 10.1 us
    slice x6 -> x17, local copies, waits for them, and re-layouts: 585 us -> 13.3 us  [the longest x10 7.12 us: side_strips(): part[..., -width:]]
    dot_general x4, matrix products: 238 us -> 103 us  [the longest x2 52.5 us: by_rows(): jnp.einsum('ik,kj->ij', row_kernel, gathered, precision=lax.Precision.HIGH)]
    concatenate x3 -> x6, local copies, waits for them, and re-layouts: 79.5 us -> 2.84 us  [the longest x2 2.31 us: side_strips(): both = jnp.concatenate([left, right], axis=2)]
    all_gather x2 -> x4, waiting for transfers between devices: 453 us -> 409 us  [the longest x2 246 us: by_rows(): gathered = lax.all_gather(field, 'gx', axis=0, tiled=True)]
    pallas_call x0 -> x2, Pallas kernels: none -> 42.9 us  [the longest x1 24.8 us: forward(): pl.pallas_call(forward_kernel, grid=(rhs, rows // BAND), in_specs=banded_...]
    another operation x1 -> x0, local copies, waits for them, and re-layouts: 28.7 us -> none  [forward_rows(): stacked = jnp.stack([first, second], axis=2)]
    another operation x2 -> x3, other arithmetic: 33.9 us -> 5.98 us  [body(): return forward(jnp.stack([one, two]), noise_var, observed)]
    ppermute x8, waiting for transfers between devices: 21.3 us -> 0.68 us  [the longest x2 0.65 us: side_strips(): lax.ppermute(strip_last, 'gy', [(i, i + 1) for i in range(count - 1)])]
  transfers between devices with their start and end apart: 10 -> 12, of which waited for: 6 -> 5; matrix products, arithmetic and copies ran while one was open for 1% -> 15% of each run, Pallas kernels for 0% -> 0%
where the time goes in v1:
time: 630 us; the launch traced here: 624 us
  waiting for transfers between devices  410 us (65%)
  matrix products  103 us (16%)
  Pallas kernels  42.9 us (7%)
  local copies, waits for them, and re-layouts  22.3 us (4%)
  starting transfers between devices  21.7 us (3%)
  between operations  13.7 us (2%)
  other arithmetic  10.1 us (2%)
    all_gather x2, waiting for transfers between devices, by_rows(): gathered = lax.all_gather(field, 'gx', axis=0, tiled=True)  246 us
    all_gather x2, waiting for transfers between devices, by_columns(): gathered = lax.all_gather(field, 'gy', axis=1, tiled=True)  163 us
    dot_general x2, matrix products, by_rows(): jnp.einsum('ik,kj->ij', row_kernel, gathered, precision=lax.Precision.HIGH)  52.5 us
    dot_general x2, matrix products, by_columns(): jnp.einsum('ik,jk->ij', gathered, col_kernel, precision=lax.Precision.HIGH)  50.9 us
    pallas_call x1, Pallas kernels, forward(): pl.pallas_call(forward_kernel, grid=(rhs, rows // BAND), in_specs=banded_...  24.8 us
    pallas_call x1, Pallas kernels, adjoint(): pl.pallas_call(adjoint_kernel, grid=(rhs, rows // (2 * BAND)), in_specs=b...  18.1 us
  transfers between devices with their start and end apart: 12, of which 5 were waited for; matrix products, arithmetic and copies ran while one was open for 15% of the time, Pallas kernels for 0%

profile of v1, /device:TPU:0, one launch (start us, length us, event | category | flops | bytes accessed | tf_op | source)
XLA Modules:
  0.0 624.1 jit_solution(14172235019108774605)
XLA Ops:
  6.5 0.9 fusion.48
  7.4 1.3 collective-permute-start.1
  8.7 5.6 collective-permute-start
  14.3 4.9 fusion.47
  19.6 1.2 fusion.6.col_table
  20.9 2.2 copy.22
  23.1 2.2 copy.23
  26.0 1.3 collective-permute-start.3
  27.5 3.0 collective-permute-start.2
  30.7 0.7 collective-permute-done.2
  31.4 1.9 copy.12
  33.4 1.7 pad.8.sides
  35.1 18.1 %shard_map.46 = f32[2,1024,512]{2,1,0:T(8,128)} custom-call(f32[2,2048,1024]{2,1,0:T(8,128)} %observed.1, f32[2,2048,1024]{2,1,0:T(8,128)} %observed.1, f32[2,2048,1024]{2,1,0:T(8,128)} %observed.1, f32[2,8,1024]{2,1,0:T(8,128)S(1)} %collective-permute-done.above, f32[2,8,1024]{2,1,0:T(8,128)S(1)} %collective-permute-done.1.below, ...), custom_call_target="tpu_custom_call" | custom-call | tf_op jit(solution)/shard_map/pallas_call | solution.py:125
  53.2 4.6 fusion.49
  57.8 0.7 all-gather.13.cloned.1.call-update
  58.9 92.2 %all-gather.11.cloned.1.call-done = f32[1,1024,4096]{2,1,0:T(8,128)} async-done(((f32[1,1024,512]{2,1,0:T(8,128)}), f32[1,1024,4096]{2,1,0:T(8,128)}) %all-gather.11.cloned.1.call-update) | async-done | bytes 16777232 | tf_op jit(solution)/shard_map/all_gather | solution.py:165
  151.1 19.4 %fusion = f32[1024,512]{1,0:T(8,128)} fusion(f32[512,4096]{1,0:T(8,128)} %param.7, f32[1,1024,4096]{2,1,0:T(8,128)} %all-gather.11.cloned.1.call-done), kind=kOutput, calls=%fused_computation | convolution fusion | flops 12884901888 | bytes 27262976 | tf_op jit(solution)/shard_map/ik,jk->ij/dot_general | solution.py:166
  170.5 131.8 %all-gather.13.cloned.1.call-done = f32[1,4096,512]{2,1,0:T(8,128)} async-done(((f32[1,1024,512]{2,1,0:T(8,128)}), f32[1,4096,512]{2,1,0:T(8,128)}) %all-gather.13.cloned.1.call-update) | async-done | bytes 8388624 | tf_op jit(solution)/shard_map/all_gather | solution.py:170
  302.3 33.1 %fusion.14 = f32[1024,512]{0,1:T(8,128)} fusion(f32[1024,4096]{1,0:T(8,128)} %param.6, f32[1,4096,512]{2,1,0:T(8,128)} %all-gather.13.cloned.1.call-done), kind=kOutput, calls=%fused_computation.27 | convolution fusion | flops 12884901888 | bytes 27262976 | tf_op jit(solution)/shard_map/ik,kj->ij/dot_general | solution.py:171
  336.3 1.2 fusion.9.col_table
  337.6 114.2 %all-gather.7.cloned.1.call-done = f32[4096,512]{1,0:T(8,128)} async-done(((f32[1024,512]{1,0:T(8,128)}), f32[4096,512]{1,0:T(8,128)}) %all-gather.7.cloned.1.call-update) | async-done | bytes 8388624 | tf_op jit(solution)/shard_map/all_gather | solution.py:170
  451.8 19.4 %convolution_bitcast_fusion.1 = f32[1,1024,512]{2,1,0:T(8,128)} fusion(f32[4096,512]{1,0:T(8,128)} %all-gather.7.cloned.1.call-done, f32[1024,4096]{1,0:T(8,128)} %param.6), kind=kOutput, calls=%fused_computation.29 | convolution fusion | flops 12884901888 | bytes 27262976 | tf_op jit(solution)/shard_map/ik,kj->ij/dot_general | solution.py:171
  471.2 70.5 %all-gather.9.cloned.1.call-done = f32[1024,4096]{0,1:T(8,128)} async-done(((f32[1024,512]{0,1:T(8,128)}), f32[1024,4096]{0,1:T(8,128)}) %all-gather.9.cloned.1.call-update) | async-done | bytes 16777232 | tf_op jit(solution)/shard_map/all_gather | solution.py:165
  541.6 31.5 %convolution_bitcast_fusion = f32[1,1024,512]{2,1,0:T(8,128)S(1)} fusion(f32[1024,4096]{0,1:T(8,128)} %all-gather.9.cloned.1.call-done, f32[512,4096]{1,0:T(8,128)} %param.7), kind=kOutput, calls=%fused_computation.28 | convolution fusion | flops 12884901888 | bytes 27262976 | tf_op jit(solution)/shard_map/ik,jk->ij/dot_general | solution.py:166
  573.2 1.3 collective-permute-start.5
  574.5 1.4 fusion.17
  575.9 4.5 collective-permute-start.4
  580.4 1.6 copy.15
  583.0 1.3 collective-permute-start.7
  584.4 3.0 collective-permute-start.6
  587.4 4.6 pad_maximum_fusion.main.before.after
  592.5 24.8 %shard_map.47 = f32[2,2048,1024]{2,1,0:T(8,128)} custom-call(f32[2,1024,512]{2,1,0:T(8,128)} %pad_maximum_fusion.main.before.after, f32[2,1024,512]{2,1,0:T(8,128)} %pad_maximum_fusion.main.before.after, f32[2,1024,512]{2,1,0:T(8,128)} %pad_maximum_fusion.main.before.after, f32[2,8,512]{2,1,0:T(8,128)S(1)} %collective-permute-done.4.above, ...), custom_call_target="tpu_custom_call" | custom-call | tf_op jit(solution)/shard_map/pallas_call | solution.py:144
  (50 shorter events, 4.4 us)
Async XLA Ops:
  6.5 144.5 %all-gather.11.cloned.1.call-start = ((), (), s32[]{:S(2)}) async-start(), calls=%async_computation.2 | async-start | bytes 18874368 | tf_op jit(solution)/shard_map/all_gather | solution.py:165
  7.4 17.9 %collective-permute-start.1 = (f32[2,8,1024]{2,1,0:T(8,128)S(1)}, f32[2,8,1024]{2,1,0:T(8,128)S(1)}, u32[]{:S(2)}, u32[]{:S(2)}) collective-permute-start(f32[2,8,1024]{2,1,0:T(8,128)S(1)} %get-tuple-element.7), channel_id=1, source_target_pairs={{8,0},{16,8},{24,16},{9,1},{17,9},{25,17},{10,2},{18,10},{26,18},{... | collective-permute-start | bytes 196616 | tf_op jit(solution)/shard_map/ppermute | solution.py:40
  8.7 16.9 %collective-permute-start = (f32[2,8,1024]{2,1,0:T(8,128)S(1)}, f32[2,8,1024]{2,1,0:T(8,128)S(1)}, u32[]{:S(2)}, u32[]{:S(2)}) collective-permute-start(f32[2,8,1024]{2,1,0:T(8,128)S(1)} %get-tuple-element.8), channel_id=1, source_target_pairs={{0,8},{8,16},{16,24},{1,9},{9,17},{17,25},{2,10},{10,18},{18,26},{... | collective-permute-start | bytes 196616 | tf_op jit(solution)/shard_map/ppermute | solution.py:39
  26.0 4.7 collective-permute-start.3
  27.5 3.9 collective-permute-start.2
  57.8 244.5 %all-gather.13.cloned.1.call-start = ((), (), s32[]{:S(2)}) async-start(), calls=%async_computation.3 | async-start | bytes 10485760 | tf_op jit(solution)/shard_map/all_gather | solution.py:170
  58.5 393.3 %all-gather.7.cloned.1.call-start = ((), (), s32[]{:S(2)}) async-start(), calls=%async_computation | async-start | bytes 10485760 | tf_op jit(solution)/shard_map/all_gather | solution.py:170
  170.5 371.2 %all-gather.9.cloned.1.call-start = ((), (), s32[]{:S(2)}) async-start(), calls=%async_computation.1 | async-start | bytes 18874368 | tf_op jit(solution)/shard_map/all_gather | solution.py:165
  541.6 31.5 %copy-start = (f32[1,1024,512]{2,1,0:T(8,128)S(1)}, f32[1,1024,512]{2,1,0:T(8,128)}, u32[]{:S(2)}) copy-start(f32[1,1024,512]{2,1,0:T(8,128)} %convolution_bitcast_fusion.1) | copy-start | bytes 6291460
  573.2 1.3 copy-start.1
  573.2 9.1 %collective-permute-start.5 = (f32[2,8,512]{2,1,0:T(8,128)S(1)}, f32[2,8,512]{2,1,0:T(8,128)S(1)}, u32[]{:S(2)}, u32[]{:S(2)}) collective-permute-start(f32[2,8,512]{2,1,0:T(8,128)S(1)} %get-tuple-element.11), channel_id=1, source_target_pairs={{8,0},{16,8},{24,16},{9,1},{17,9},{25,17},{10,2},{18,10},{26,18},{... | collective-permute-start | bytes 98312 | tf_op jit(solution)/shard_map/ppermute | solution.py:40
  575.9 6.7 %collective-permute-start.4 = (f32[2,8,512]{2,1,0:T(8,128)S(1)}, f32[2,8,512]{2,1,0:T(8,128)S(1)}, u32[]{:S(2)}, u32[]{:S(2)}) collective-permute-start(f32[2,8,512]{2,1,0:T(8,128)S(1)} %get-tuple-element.12), channel_id=1, source_target_pairs={{0,8},{8,16},{16,24},{1,9},{9,17},{17,25},{2,10},{10,18},{18,26},{... | collective-permute-start | bytes 98312 | tf_op jit(solution)/shard_map/ppermute | solution.py:39
  583.0 9.1 %collective-permute-start.7 = (f32[2,1040,2]{1,2,0:T(2,128)S(1)}, f32[2,1040,2]{1,2,0:T(2,128)S(1)}, u32[]{:S(2)}, u32[]{:S(2)}) collective-permute-start(f32[2,1040,2]{1,2,0:T(2,128)S(1)} %concatenate.22), channel_id=1, source_target_pairs={{1,0},{2,1},{3,2},{4,3},{5,4},{6,5},{7,6},{9,8},{10,9},{11,10},{12... | collective-permute-start | bytes 49928 | tf_op jit(solution)/shard_map/ppermute | solution.py:49
  584.4 7.7 %collective-permute-start.6 = (f32[2,1040,2]{1,2,0:T(2,128)S(1)}, f32[2,1040,2]{1,2,0:T(2,128)S(1)}, u32[]{:S(2)}, u32[]{:S(2)}) collective-permute-start(f32[2,1040,2]{1,2,0:T(2,128)S(1)} %concatenate.21), channel_id=1, source_target_pairs={{0,1},{1,2},{2,3},{3,4},{4,5},{5,6},{6,7},{8,9},{9,10},{10,11},{11... | collective-permute-start | bytes 49928 | tf_op jit(solution)/shard_map/ppermute | solution.py:48
Sparse Core Ops, SparseCore 0:
  57.9 93.1 all-gather.10
  152.6 149.6 all-gather.12
  303.9 147.8 all-gather.6
  453.5 88.0 all-gather.8

commit v2 on v1

--- a/solution.py
+++ b/solution.py
@@ -97,21 +97,25 @@
     out[0] = exact_left(row_table[...], cols) + noise[...] * observed[0]
 
 
-def banded_specs(rows, cols, band):
+def banded_specs(rows, cols, band, source):
     per = band // PAD
     last = rows // PAD - 1
     return [
-        pl.BlockSpec((1, band, cols), lambda r, i: (r, i, 0)),
-        pl.BlockSpec((1, PAD, cols), lambda r, i: (r, jnp.maximum(i * per - 1, 0), 0)),
-        pl.BlockSpec((1, PAD, cols), lambda r, i: (r, jnp.minimum((i + 1) * per, last), 0)),
-        pl.BlockSpec((1, PAD, cols), lambda r, i: (r, 0, 0)),
-        pl.BlockSpec((1, PAD, cols), lambda r, i: (r, 0, 0)),
-        pl.BlockSpec((1, rows + 2 * PAD, 128), lambda r, i: (r, 0, 0)),
+        pl.BlockSpec((1, band, cols), lambda r, i: (source, i, 0)),
+        pl.BlockSpec((1, PAD, cols), lambda r, i: (source, jnp.maximum(i * per - 1, 0), 0)),
+        pl.BlockSpec((1, PAD, cols), lambda r, i: (source, jnp.minimum((i + 1) * per, last), 0)),
+        pl.BlockSpec((1, PAD, cols), lambda r, i: (source, 0, 0)),
+        pl.BlockSpec((1, PAD, cols), lambda r, i: (source, 0, 0)),
+        pl.BlockSpec((1, rows + 2 * PAD, 128), lambda r, i: (source, 0, 0)),
     ]
 
 
 def whole(table):
     return pl.BlockSpec(table.shape, lambda r, i: (0, 0))
+
+
+def cost(flops, moved):
+    return pl.CostEstimate(flops=flops, bytes_accessed=moved, transcendentals=0)
 
 
 def adjoint(observed):
@@ -122,43 +126,64 @@
     row_table = weights(positions(BAND, 0)[:, None], positions(2 * BAND + 2 * PAD, -PAD)[None, :])
     col_table = weights(positions(coarse, 0)[None, :], positions(cols, 0)[:, None])
     side_table = weights(positions(coarse, 0)[None, :], halo_positions(4, cols)[:, None])
-    return pl.pallas_call(
-        adjoint_kernel,
-        grid=(rhs, rows // (2 * BAND)),
-        in_specs=banded_specs(rows, cols, 2 * BAND)
-        + [whole(row_table), whole(col_table), whole(side_table)],
-        out_specs=pl.BlockSpec((1, BAND, coarse), lambda r, i: (r, i, 0)),
-        out_shape=jax.ShapeDtypeStruct((rhs, rows // 2, coarse), jnp.float32),
-        compiler_params=pltpu.CompilerParams(vmem_limit_bytes=VMEM_BYTES),
-    )(observed, observed, observed, above, below, sides, row_table, col_table, side_table)
-
-
-def forward(product, noise_var, observed):
-    rhs, rows, cols = product.shape
+
+    def one(source, earlier):
+        table = side_table
+        if earlier is not None:
+            table, _ = lax.optimization_barrier((side_table, earlier))
+        return pl.pallas_call(
+            adjoint_kernel,
+            grid=(1, rows // (2 * BAND)),
+            in_specs=banded_specs(rows, cols, 2 * BAND, source)
+            + [whole(row_table), whole(col_table), whole(side_table)],
+            out_specs=pl.BlockSpec((1, BAND, coarse), lambda r, i: (0, i, 0)),
+            out_shape=jax.ShapeDtypeStruct((1, rows // 2, coarse), jnp.float32),
+            compiler_params=pltpu.CompilerParams(vmem_limit_bytes=VMEM_BYTES),
+            cost_estimate=cost(4 * rows * cols * (BAND + coarse), 5 * rows * cols),
+        )(observed, observed, observed, above, below, sides, row_table, col_table, table)[0]
+
+    return one
+
+
+def forward(product, target, noise_var, observed, partial):
+    product = product[None]
+    _, rows, cols = product.shape
     above, below = neighbours(product, "gx", 1, PAD)
     sides = side_strips(product, above, below, 2)
     fine = 2 * cols
     row_table = weights(positions(BAND + 2 * PAD, -PAD)[None, :], positions(2 * BAND, 0)[:, None])
     col_table = weights(positions(cols, 0)[:, None], positions(fine, 0)[None, :])
     side_table = weights(halo_positions(2, cols)[:, None], positions(fine, 0)[None, :])
-    return pl.pallas_call(
-        forward_kernel,
-        grid=(rhs, rows // BAND),
-        in_specs=banded_specs(rows, cols, BAND)
-        + [
-            whole(row_table),
-            whole(col_table),
-            whole(side_table),
-            pl.BlockSpec((2 * BAND, fine), lambda r, i: (i, 0)),
-            pl.BlockSpec((1, 2 * BAND, fine), lambda r, i: (r, i, 0)),
-        ],
-        out_specs=pl.BlockSpec((1, 2 * BAND, fine), lambda r, i: (r, i, 0)),
-        out_shape=jax.ShapeDtypeStruct((rhs, 2 * rows, fine), jnp.float32),
-        compiler_params=pltpu.CompilerParams(vmem_limit_bytes=VMEM_BYTES),
-    )(
+    operands = [
         product, product, product, above, below, sides,
         row_table, col_table, side_table, noise_var, observed,
-    )
+    ]
+    in_specs = banded_specs(rows, cols, BAND, 0) + [
+        whole(row_table),
+        whole(col_table),
+        whole(side_table),
+        pl.BlockSpec((2 * BAND, fine), lambda r, i: (i, 0)),
+        pl.BlockSpec((1, 2 * BAND, fine), lambda r, i: (target, i, 0)),
+    ]
+    kernel, aliases = forward_kernel, {}
+    if partial is not None:
+        aliases = {len(operands): 0}
+        operands.append(partial)
+        in_specs.append(pl.BlockSpec(memory_space=pl.ANY))
+
+        def kernel(*refs):
+            forward_kernel(*refs[:11], refs[12])
+
+    return pl.pallas_call(
+        kernel,
+        grid=(1, rows // BAND),
+        in_specs=in_specs,
+        out_specs=pl.BlockSpec((1, 2 * BAND, fine), lambda r, i: (target, i, 0)),
+        out_shape=jax.ShapeDtypeStruct(observed.shape, jnp.float32),
+        input_output_aliases=aliases,
+        compiler_params=pltpu.CompilerParams(vmem_limit_bytes=VMEM_BYTES),
+        cost_estimate=cost(4 * rows * fine * (cols + 2 * BAND), 26 * rows * fine),
+    )(*operands)
 
 
 def by_columns(field, col_kernel):
@@ -166,16 +191,46 @@
     return jnp.einsum("ik,jk->ij", gathered, col_kernel, precision=lax.Precision.HIGH)
 
 
-def by_rows(field, row_kernel):
-    gathered = lax.all_gather(field, "gx", axis=0, tiled=True)
-    return jnp.einsum("ik,kj->ij", row_kernel, gathered, precision=lax.Precision.HIGH)
+def exchange(field):
+    count = lax.axis_size("gx")
+    from_left, from_right = [field], [field]
+    for step in range(1, count):
+        up = [(i, i + 1) for i in range(step - 1, count - 1)]
+        down = [(i + 1, i) for i in range(count - step)]
+        from_left.append(lax.ppermute(from_left[-1], "gx", up))
+        from_right.append(lax.ppermute(from_right[-1], "gx", down))
+    return from_left, from_right
+
+
+def row_products(from_left, from_right, row_kernel):
+    count, place = lax.axis_size("gx"), lax.axis_index("gx")
+    depth = from_left[0].shape[0]
+    total = None
+    for step in range(count):
+        block = from_left[0]
+        if step:
+            block = jnp.where(place + step < count, from_right[step], from_left[count - step])
+        owner = lax.rem(place + step, count)
+        part = lax.dynamic_slice_in_dim(row_kernel, owner * depth, depth, axis=1)
+        term = jnp.einsum("ik,kj->ij", part, block, precision=lax.Precision.HIGH)
+        total = term if total is None else total + term
+    return total
 
 
 def body(observed, noise_var, row_kernel, col_kernel):
     inducing = adjoint(observed)
-    one = by_rows(by_columns(inducing[0], col_kernel), row_kernel)
-    two = by_columns(by_rows(inducing[1], row_kernel), col_kernel)
-    return forward(jnp.stack([one, two]), noise_var, observed)
+    rows_first = inducing(1, None)
+    cols_first = inducing(0, rows_first)
+    from_left, from_right = exchange(rows_first)
+    mixed_cols = by_columns(cols_first, col_kernel)
+    from_left[-1], from_right[-1], mixed_cols = lax.optimization_barrier(
+        (from_left[-1], from_right[-1], mixed_cols)
+    )
+    again = exchange(mixed_cols)
+    two = by_columns(row_products(from_left, from_right, row_kernel), col_kernel)
+    partial = forward(two, 1, noise_var, observed, None)
+    one = row_products(*again, row_kernel)
+    return forward(one, 0, noise_var, observed, partial)
 
 
 def solution(mesh):

time: 630 us -> 508 us (0.81)
  waiting for transfers between devices: 410 us -> 233 us
  local copies, waits for them, and re-layouts: 22.3 us -> 57.1 us
  starting transfers between devices: 21.7 us -> 54.6 us
  matrix products: 103 us -> 85 us
    all_gather x2 -> x0, waiting for transfers between devices: 246 us -> none  [by_rows(): gathered = lax.all_gather(field, 'gx', axis=0, tiled=True)]
    ppermute x0 -> x12, waiting for transfers between devices: none -> 233 us  [the longest x6 190 us: exchange(): from_right.append(lax.ppermute(from_right[-1], 'gx', down))]
    all_gather x2, waiting for transfers between devices: 163 us -> 0.01 us  [by_columns(): gathered = lax.all_gather(field, 'gy', axis=1, tiled=True)]
    ppermute x0 -> x12, starting transfers between devices: none -> 20.7 us  [the longest x6 13 us: exchange(): from_left.append(lax.ppermute(from_left[-1], 'gx', up))]
    dot_general x2, matrix products: 50.9 us -> 37.1 us  [by_columns(): jnp.einsum('ik,jk->ij', gathered, col_kernel, precision=lax.Precision.HIGH)]
    slice x10 -> x17, local copies, waits for them, and re-layouts: 7.12 us -> 20.7 us  [side_strips(): part[..., -width:]]
    slice x5 -> x8, local copies, waits for them, and re-layouts: 0.68 us -> 9.13 us  [side_strips(): part[..., :width]]
    ppermute x2 -> x3, starting transfers between devices: 10.1 us -> 15.8 us  [neighbours(): before = lax.ppermute(tail, axis, [(i, i + 1) for i in range(count - 1)])]
  transfers between devices with their start and end apart: 12 -> 26, of which waited for: 5 -> 8; matrix products, arithmetic and copies ran while one was open for 15% -> 24% of each run, Pallas kernels for 0% -> 0%
where the time goes in v2:
time: 508 us; the launch traced here: 499 us
  waiting for transfers between devices  233 us (46%)
  matrix products  85 us (17%)
  local copies, waits for them, and re-layouts  57.1 us (11%)
  starting transfers between devices  54.6 us (11%)
  Pallas kernels  46.5 us (9%)
  between operations  14.3 us (3%)
  other arithmetic  8.1 us (2%)
    ppermute x6, waiting for transfers between devices, exchange(): from_right.append(lax.ppermute(from_right[-1], 'gx', down))  190 us
    dot_general x8, matrix products, row_products(): term = jnp.einsum('ik,kj->ij', part, block, precision=lax.Precision.HIGH)  47.9 us
    ppermute x6, waiting for transfers between devices, exchange(): from_left.append(lax.ppermute(from_left[-1], 'gx', up))  43.4 us
    dot_general x2, matrix products, by_columns(): jnp.einsum('ik,jk->ij', gathered, col_kernel, precision=lax.Precision.HIGH)  37.1 us
    pallas_call x2, Pallas kernels, forward(): pl.pallas_call(kernel, grid=(1, rows // BAND), in_specs=in_specs, out_spe...  26.7 us
    slice x17, local copies, waits for them, and re-layouts, side_strips(): part[..., -width:]  20.7 us
    pallas_call x2, Pallas kernels, one(): pl.pallas_call(adjoint_kernel, grid=(1, rows // (2 * BAND)), in_specs=ban...  19.8 us
    ppermute x3, starting transfers between devices, neighbours(): before = lax.ppermute(tail, axis, [(i, i + 1) for i in range(count - 1)])  15.8 us
  transfers between devices with their start and end apart: 26, of which 8 were waited for; matrix products, arithmetic and copies ran while one was open for 24% of the time, Pallas kernels for 0%

profile of v2, /device:TPU:0, one launch (start us, length us, event | category | flops | bytes accessed | tf_op | source)
XLA Modules:
  0.0 498.7 jit_solution(1139797906524673052)
XLA Ops:
  8.7 5.6 %collective-permute-start = (f32[2,8,1024]{2,1,0:T(8,128)S(1)}, f32[2,8,1024]{2,1,0:T(8,128)S(1)}, u32[]{:S(2)}, u32[]{:S(2)}) collective-permute-start(f32[2,8,1024]{2,1,0:T(8,128)S(1)} %get-tuple-element.16), channel_id=1, source_target_pairs={{0,8},{8,16},{16,24},{1,9},{9,17},{17,25},{2,10},{10,18},{18,26},{... | collective-permute-start | bytes 196616 | tf_op jit(solution)/shard_map/ppermute | solution.py:39
  14.3 4.9 fusion.83
  20.9 2.2 copy.27
  23.1 2.2 copy.28
  27.5 3.0 collective-permute-start.2
  36.0 9.5 %shard_map.46 = f32[1,1024,512]{2,1,0:T(8,128)S(1)} custom-call(f32[2,2048,1024]{2,1,0:T(8,128)} %refs_10_.1, f32[2,2048,1024]{2,1,0:T(8,128)} %refs_10_.1, f32[2,2048,1024]{2,1,0:T(8,128)} %refs_10_.1, f32[2,8,1024]{2,1,0:T(8,128)S(1)} %copy-done.6, f32[2,8,1024]{2,1,0:T(8,128)S(1)} %collective-permute-done.1.below, f32[2,2064,128]{2,1,0:T(8,128)S(1)} %pad.11.sides, ...), custom_call_target="tpu_custom_call" | custom-call | flops 6442450944 | bytes 10485760 | tf_op jit(solution)/shard_map/pallas_call | solution.py:134
  45.5 10.4 %shard_map.47 = f32[1,1024,512]{2,1,0:T(8,128)} custom-call(f32[2,2048,1024]{2,1,0:T(8,128)} %refs_10_.1, f32[2,2048,1024]{2,1,0:T(8,128)} %refs_10_.1, f32[2,2048,1024]{2,1,0:T(8,128)} %refs_10_.1, f32[2,8,1024]{2,1,0:T(8,128)S(1)} %copy-done.6, f32[2,8,1024]{2,1,0:T(8,128)S(1)} %collective-permute-done.1.below, f32[2,2064,128]{2,1,0:T(8,128)S(1)} %pad.11.sides, ...), custom_call_target="tpu_custom_call" | custom-call | flops 6442450944 | bytes 10485760 | tf_op jit(solution)/shard_map/pallas_call | solution.py:134
  57.2 5.9 %collective-permute-start.4 = (f32[1024,512]{1,0:T(8,128)S(1)}, f32[1024,512]{1,0:T(8,128)}, u32[]{:S(2)}, u32[]{:S(2)}) collective-permute-start(f32[1024,512]{1,0:T(8,128)S(1)} %bitcast.15), channel_id=1, source_target_pairs={{0,8},{8,16},{16,24},{1,9},{9,17},{17,25},{2,10},{10,18},{18,26},{... | collective-permute-start | bytes 6291464 | tf_op jit(solution)/shard_map/ppermute | solution.py:200
  63.1 42.3 %collective-permute-done.7 = f32[1024,512]{1,0:T(8,128)} collective-permute-done((f32[1024,512]{1,0:T(8,128)S(1)}, f32[1024,512]{1,0:T(8,128)}, u32[]{:S(2)}, u32[]{:S(2)}) %collective-permute-start.7) | collective-permute-done | bytes 2097184 | tf_op jit(solution)/shard_map/ppermute | solution.py:201
  107.1 2.0 collective-permute-start.5
  109.1 47.5 %collective-permute-done.8 = f32[1024,512]{1,0:T(8,128)} collective-permute-done((f32[1024,512]{1,0:T(8,128)}, f32[1024,512]{1,0:T(8,128)}, u32[]{:S(2)}, u32[]{:S(2)}) %collective-permute-start.8) | collective-permute-done | bytes 2097184 | tf_op jit(solution)/shard_map/ppermute | solution.py:201
  159.8 7.0 %fusion.14 = f32[1024,512]{1,0:T(8,128)} fusion(f32[1024,4096]{1,0:T(8,128)} %param.6, s32[]{:T(128)S(6)} %select_n.166, f32[1,1024,512]{2,1,0:T(8,128)S(1)} %shard_map.46), kind=kOutput, calls=%fused_computation.14 | convolution fusion | flops 3221225472 | bytes 8388612 | tf_op jit(solution)/shard_map/ik,kj->ij/dot_general | solution.py:215
  166.9 18.8 %fusion = f32[1024,512]{1,0:T(8,128)S(1)} fusion(f32[512,4096]{1,0:T(8,128)} %param.7, f32[1,1024,4096]{2,1,0:T(8,128)} %all-gather.6.cloned.1.call-done), kind=kOutput, calls=%fused_computation | convolution fusion | flops 12884901888 | bytes 27262976 | tf_op jit(solution)/shard_map/ik,jk->ij/dot_general | solution.py:191
  185.6 20.7 %collective-permute-done.9 = f32[1024,512]{1,0:T(8,128)} collective-permute-done((f32[1024,512]{1,0:T(8,128)}, f32[1024,512]{1,0:T(8,128)}, u32[]{:S(2)}, u32[]{:S(2)}) %collective-permute-start.9) | collective-permute-done | bytes 2097184 | tf_op jit(solution)/shard_map/ppermute | solution.py:201
  206.4 6.0 %fusion.10 = f32[1024,512]{1,0:T(8,128)S(1)} fusion(f32[1024,4096]{1,0:T(8,128)} %param.6, s32[]{:T(128)S(6)} %select_n.175, f32[1024,512]{1,0:T(8,128)} %collective-permute-done.7, f32[1024,512]{1,0:T(8,128)} %collective-permute-done.6, pred[]{:T(512)S(6)} %lt.145), kind=kOutput, calls=%fused_computation.10 | convolution fusion | flops 3221749760 | bytes 10485765 | tf_op jit(solution)/shard_map/ik,kj->ij/dot_general | solution.py:215
  212.4 6.2 %fusion.2 = f32[1024,512]{1,0:T(8,128)S(1)} fusion(f32[1024,4096]{1,0:T(8,128)S(1)} %bitcast.17, s32[]{:T(128)S(6)} %select_n.181, f32[1024,512]{1,0:T(8,128)} %collective-permute-done.9, f32[1024,512]{1,0:T(8,128)} %collective-permute-done.4, pred[]{:T(512)S(6)} %lt.149), kind=kOutput, calls=%fused_computation.2 | convolution fusion | flops 3221749760 | bytes 10485765 | tf_op jit(solution)/shard_map/ik,kj->ij/dot_general | solution.py:215
  218.6 6.7 %add_add_fusion = f32[1024,512]{1,0:T(8,128)} fusion(f32[1024,512]{1,0:T(8,128)S(1)} %fusion.2, f32[1024,512]{1,0:T(8,128)S(1)} %copy-done.9, f32[1024,512]{1,0:T(8,128)S(1)} %fusion.10, f32[1024,512]{1,0:T(8,128)} %collective-permute-done.8, f32[1024,512]{1,0:T(8,128)} %collective-permute-done.5, f32[1024,4096]{1,0:T(8,128)S(1)} %bitcast.17, ...), kind=kOutput, calls=%fused_computation.27 | convolution fusion | flops 3223322624 | bytes 16777220 | tf_op jit(solution)/shard_map/ik,kj->ij/dot_general | solution.py:215
  228.3 43.0 %collective-permute-done.11 = f32[1024,512]{1,0:T(8,128)S(1)} collective-permute-done((f32[1024,512]{1,0:T(8,128)S(1)}, f32[1024,512]{1,0:T(8,128)S(1)}, u32[]{:S(2)}, u32[]{:S(2)}) %collective-permute-start.11) | collective-permute-done | bytes 2097184 | tf_op jit(solution)/shard_map/ppermute | solution.py:200
  272.0 7.1 %collective-permute-done.10 = f32[1024,512]{1,0:T(8,128)S(1)} collective-permute-done((f32[1024,512]{1,0:T(8,128)S(1)}, f32[1024,512]{1,0:T(8,128)S(1)}, u32[]{:S(2)}, u32[]{:S(2)}) %collective-permute-start.10) | collective-permute-done | bytes 2097184 | tf_op jit(solution)/shard_map/ppermute | solution.py:201
  281.2 46.0 %collective-permute-done.14 = f32[1024,512]{1,0:T(8,128)S(1)} collective-permute-done((f32[1024,512]{1,0:T(8,128)S(1)}, f32[1024,512]{1,0:T(8,128)S(1)}, u32[]{:S(2)}, u32[]{:S(2)}) %collective-permute-start.14) | collective-permute-done | bytes 2097184 | tf_op jit(solution)/shard_map/ppermute | solution.py:201
  331.4 5.6 %fusion.16 = f32[1024,512]{1,0:T(8,128)S(1)} fusion(f32[1024,512]{1,0:T(8,128)S(1)} %fusion, f32[1024,4096]{1,0:T(8,128)} %param.6, s32[]{:T(128)S(6)} %select_n.166), kind=kOutput, calls=%fused_computation.16 | convolution fusion | flops 3221225472 | bytes 8388612 | tf_op jit(solution)/shard_map/ik,kj->ij/dot_general | solution.py:215
  337.0 5.5 %fusion.8 = f32[1024,512]{1,0:T(8,128)S(1)} fusion(f32[1024,4096]{1,0:T(8,128)} %param.6, s32[]{:T(128)S(6)} %select_n.178, f32[1024,512]{1,0:T(8,128)S(1)} %collective-permute-done.14, f32[1024,512]{1,0:T(8,128)S(1)} %collective-permute-done.12, pred[]{:T(512)S(6)} %lt.147), kind=kOutput, calls=%fused_computation.8 | convolution fusion | flops 3221749760 | bytes 10485765 | tf_op jit(solution)/shard_map/ik,kj->ij/dot_general | solution.py:215
  342.5 5.3 %fusion.12 = f32[1024,512]{1,0:T(8,128)S(1)} fusion(f32[1024,4096]{1,0:T(8,128)} %param.6, s32[]{:T(128)S(6)} %select_n.175, f32[1024,512]{1,0:T(8,128)S(1)} %collective-permute-done.10, f32[1024,512]{1,0:T(8,128)S(1)} %collective-permute-done.13, pred[]{:T(512)S(6)} %lt.145), kind=kOutput, calls=%fused_computation.12 | convolution fusion | flops 3221749760 | bytes 10485765 | tf_op jit(solution)/shard_map/ik,kj->ij/dot_general | solution.py:215
  347.8 26.1 %collective-permute-done.15 = f32[1024,512]{1,0:T(8,128)S(1)} collective-permute-done((f32[1024,512]{1,0:T(8,128)S(1)}, f32[1024,512]{1,0:T(8,128)S(1)}, u32[]{:S(2)}, u32[]{:S(2)}) %collective-permute-start.15) | collective-permute-done | bytes 2097184 | tf_op jit(solution)/shard_map/ppermute | solution.py:201
  373.9 5.6 %add_bitcast_fusion.refs_0_.refs_1_.refs_2_ = f32[1,1024,512]{2,1,0:T(8,128)S(1)} fusion(f32[1024,512]{1,0:T(8,128)S(1)} %fusion.8, f32[1024,512]{1,0:T(8,128)S(1)} %fusion.16, f32[1024,512]{1,0:T(8,128)S(1)} %fusion.12, f32[1024,512]{1,0:T(8,128)S(1)} %collective-permute-done.15, f32[1024,512]{1,0:T(8,128)S(1)} %collective-permute-done.11, ...), kind=kOutput, calls=%fused_computation.33 | convolution fusion | flops 3223322624 | bytes 16777220 | tf_op jit(solution)/shard_map/ik,kj->ij/dot_general | solution.py:215
  382.6 5.1 %collective-permute-start.16 = (f32[1,8,512]{2,1,0:T(8,128)}, f32[1,8,512]{2,1,0:T(8,128)}, u32[]{:S(2)}, u32[]{:S(2)}) collective-permute-start(f32[1,8,512]{2,1,0:T(8,128)} %get-tuple-element.24), channel_id=1, source_target_pairs={{0,8},{8,16},{16,24},{1,9},{9,17},{17,25},{2,10},{10,18},{18,26},{... | collective-permute-start | bytes 49160 | tf_op jit(solution)/shard_map/ppermute | solution.py:39
  402.9 3.6 collective-permute-start.18
  406.5 18.4 %convolution_bitcast_fusion.main.before.after = f32[1,1024,512]{2,1,0:T(8,128)S(1)} fusion(f32[1024,4096]{1,0:T(8,128)} %all-gather.4.cloned.1.call-done, f32[512,4096]{1,0:T(8,128)} %param.7), kind=kOutput, calls=%fused_computation.40 | convolution fusion | flops 12884901888 | bytes 27262976 | tf_op jit(solution)/shard_map/ik,jk->ij/dot_general | solution.py:191
  429.3 5.1 %collective-permute-start.20 = (f32[1,8,512]{2,1,0:T(8,128)}, f32[1,8,512]{2,1,0:T(8,128)}, u32[]{:S(2)}, u32[]{:S(2)}) collective-permute-start(f32[1,8,512]{2,1,0:T(8,128)} %get-tuple-element.20), channel_id=1, source_target_pairs={{0,8},{8,16},{16,24},{1,9},{9,17},{17,25},{2,10},{10,18},{18,26},{... | collective-permute-start | bytes 49160 | tf_op jit(solution)/shard_map/ppermute | solution.py:39
  449.5 3.6 collective-permute-start.22
  464.8 13.3 %shard_map.48.refs_11_ = f32[2,2048,1024]{2,1,0:T(8,128)} custom-call(f32[1,1024,512]{2,1,0:T(8,128)S(1)} %copy-done.1, f32[1,1024,512]{2,1,0:T(8,128)S(1)} %copy-done.1, f32[1,1024,512]{2,1,0:T(8,128)S(1)} %copy-done.1, f32[1,8,512]{2,1,0:T(8,128)} %collective-permute-done.20.above, f32[1,8,512]{2,1,0:T(8,128)S(1)} %collective-permute-done.21.below, ...), custom_call_target="tpu_custom_call" | custom-call | flops 4294967296 | bytes 27262976 | tf_op jit(solution)/shard_map/pallas_call | solution.py:177
  478.2 13.3 %shard_map.49 = f32[2,2048,1024]{2,1,0:T(8,128)} custom-call(f32[1,1024,512]{2,1,0:T(8,128)S(1)} %add_bitcast_fusion.refs_0_.refs_1_.refs_2_, f32[1,1024,512]{2,1,0:T(8,128)S(1)} %add_bitcast_fusion.refs_0_.refs_1_.refs_2_, f32[1,1024,512]{2,1,0:T(8,128)S(1)} %add_bitcast_fusion.refs_0_.refs_1_.refs_2_, ...), custom_call_target="tpu_custom_call", output_to_operand_aliasing={{}: (11, {})} | custom-call | flops 4294967296 | bytes 27262976 | tf_op jit(solution)/shard_map/pallas_call | solution.py:177
  (122 shorter events, 76.9 us)
Async XLA Ops:
  6.5 160.3 %all-gather.6.cloned.1.call-start = ((), (), s32[]{:S(2)}) async-start(), calls=%async_computation.1 | async-start | bytes 18874368 | tf_op jit(solution)/shard_map/all_gather | solution.py:190
  7.4 17.9 %collective-permute-start.1 = (f32[2,8,1024]{2,1,0:T(8,128)S(1)}, f32[2,8,1024]{2,1,0:T(8,128)S(1)}, u32[]{:S(2)}, u32[]{:S(2)}) collective-permute-start(f32[2,8,1024]{2,1,0:T(8,128)S(1)} %get-tuple-element.15), channel_id=1, source_target_pairs={{8,0},{16,8},{24,16},{9,1},{17,9},{25,17},{10,2},{18,10},{26,18},{... | collective-permute-start | bytes 196616 | tf_op jit(solution)/shard_map/ppermute | solution.py:40
  8.7 16.9 %collective-permute-start = (f32[2,8,1024]{2,1,0:T(8,128)S(1)}, f32[2,8,1024]{2,1,0:T(8,128)S(1)}, u32[]{:S(2)}, u32[]{:S(2)}) collective-permute-start(f32[2,8,1024]{2,1,0:T(8,128)S(1)} %get-tuple-element.16), channel_id=1, source_target_pairs={{0,8},{8,16},{16,24},{1,9},{9,17},{17,25},{2,10},{10,18},{18,26},{... | collective-permute-start | bytes 196616 | tf_op jit(solution)/shard_map/ppermute | solution.py:39
  26.0 5.4 %collective-permute-start.3 = (f32[2,2064,4]{1,2,0:T(4,128)S(1)}, f32[2,2064,4]{1,2,0:T(4,128)S(1)}, u32[]{:S(2)}, u32[]{:S(2)}) collective-permute-start(f32[2,2064,4]{1,2,0:T(4,128)S(1)} %concatenate.28), channel_id=1, source_target_pairs={{1,0},{2,1},{3,2},{4,3},{5,4},{6,5},{7,6},{9,8},{10,9},{11,10},{12... | collective-permute-start | bytes 198152 | tf_op jit(solution)/shard_map/ppermute | solution.py:49
  27.5 3.9 collective-permute-start.2
  55.9 350.6 %all-gather.4.cloned.1.call-start = ((), (), s32[]{:S(2)}) async-start(), calls=%async_computation | async-start | bytes 18874368 | tf_op jit(solution)/shard_map/all_gather | solution.py:190
  55.9 49.5 %collective-permute-start.7 = (f32[1024,512]{1,0:T(8,128)S(1)}, f32[1024,512]{1,0:T(8,128)}, u32[]{:S(2)}, u32[]{:S(2)}) collective-permute-start(f32[1024,512]{1,0:T(8,128)S(1)} %bitcast.14), channel_id=1, source_target_pairs={{8,0},{16,8},{24,16},{9,1},{17,9},{25,17},{10,2},{18,10},{26,18},{... | collective-permute-start | bytes 6291464 | tf_op jit(solution)/shard_map/ppermute | solution.py:201
  57.2 49.8 %collective-permute-start.4 = (f32[1024,512]{1,0:T(8,128)S(1)}, f32[1024,512]{1,0:T(8,128)}, u32[]{:S(2)}, u32[]{:S(2)}) collective-permute-start(f32[1024,512]{1,0:T(8,128)S(1)} %bitcast.15), channel_id=1, source_target_pairs={{0,8},{8,16},{16,24},{1,9},{9,17},{17,25},{2,10},{10,18},{18,26},{... | collective-permute-start | bytes 6291464 | tf_op jit(solution)/shard_map/ppermute | solution.py:200
  105.4 51.2 %collective-permute-start.8 = (f32[1024,512]{1,0:T(8,128)}, f32[1024,512]{1,0:T(8,128)}, u32[]{:S(2)}, u32[]{:S(2)}) collective-permute-start(f32[1024,512]{1,0:T(8,128)} %collective-permute-done.7), channel_id=1, source_target_pairs={{8,0},{16,8},{9,1},{17,9},{10,2},{18,10},{11,3},{19,11},{12,4},{20... | collective-permute-start | bytes 6291464 | tf_op jit(solution)/shard_map/ppermute | solution.py:201
  107.1 50.8 %collective-permute-start.5 = (f32[1024,512]{1,0:T(8,128)}, f32[1024,512]{1,0:T(8,128)}, u32[]{:S(2)}, u32[]{:S(2)}) collective-permute-start(f32[1024,512]{1,0:T(8,128)} %collective-permute-done.4), channel_id=1, source_target_pairs={{8,16},{16,24},{9,17},{17,25},{10,18},{18,26},{11,19},{19,27},{12,... | collective-permute-start | bytes 6291464 | tf_op jit(solution)/shard_map/ppermute | solution.py:200
  156.6 49.8 %collective-permute-start.9 = (f32[1024,512]{1,0:T(8,128)}, f32[1024,512]{1,0:T(8,128)}, u32[]{:S(2)}, u32[]{:S(2)}) collective-permute-start(f32[1024,512]{1,0:T(8,128)} %collective-permute-done.8), channel_id=1, source_target_pairs={{8,0},{9,1},{10,2},{11,3},{12,4},{13,5},{14,6},{15,7}} | collective-permute-start | bytes 6291464 | tf_op jit(solution)/shard_map/ppermute | solution.py:201
  157.9 48.5 %collective-permute-start.6 = (f32[1024,512]{1,0:T(8,128)}, f32[1024,512]{1,0:T(8,128)}, u32[]{:S(2)}, u32[]{:S(2)}) collective-permute-start(f32[1024,512]{1,0:T(8,128)} %collective-permute-done.5), channel_id=1, source_target_pairs={{16,24},{17,25},{18,26},{19,27},{20,28},{21,29},{22,30},{23,31}} | collective-permute-start | bytes 6291464 | tf_op jit(solution)/shard_map/ppermute | solution.py:200
  166.9 45.5 %slice-start = ((s8[16777216]{0:T(1024)(128)(4,1)}), s8[4194304]{0:T(1024)(128)(4,1)S(1)}, s32[]{:S(2)}) async-start(s8[16777216]{0:T(1024)(128)(4,1)} %bitcast.16), calls=%async_computation.2 | async-start | bytes 8388608
  166.9 45.5 %slice-start.1 = ((s8[16777216]{0:T(1024)(128)(4,1)}), s8[4194304]{0:T(1024)(128)(4,1)S(1)}, s32[]{:S(2)}) async-start(s8[16777216]{0:T(1024)(128)(4,1)} %bitcast.16), calls=%async_computation.3 | async-start | bytes 8388608
  166.9 45.5 %slice-start.2 = ((s8[16777216]{0:T(1024)(128)(4,1)}), s8[4194304]{0:T(1024)(128)(4,1)S(1)}, s32[]{:S(2)}) async-start(s8[16777216]{0:T(1024)(128)(4,1)} %bitcast.16), calls=%async_computation.4 | async-start | bytes 8388608
  185.6 26.8 %slice-start.3 = ((s8[16777216]{0:T(1024)(128)(4,1)}), s8[4194304]{0:T(1024)(128)(4,1)S(1)}, s32[]{:S(2)}) async-start(s8[16777216]{0:T(1024)(128)(4,1)} %bitcast.16), calls=%async_computation.5 | async-start | bytes 8388608
  225.4 45.8 %collective-permute-start.11 = (f32[1024,512]{1,0:T(8,128)S(1)}, f32[1024,512]{1,0:T(8,128)S(1)}, u32[]{:S(2)}, u32[]{:S(2)}) collective-permute-start(f32[1024,512]{1,0:T(8,128)S(1)} %fusion), channel_id=1, source_target_pairs={{0,8},{8,16},{16,24},{1,9},{9,17},{17,25},{2,10},{10,18},{18,26},{... | collective-permute-start | bytes 6291464 | tf_op jit(solution)/shard_map/ppermute | solution.py:200
  227.0 52.2 %collective-permute-start.10 = (f32[1024,512]{1,0:T(8,128)S(1)}, f32[1024,512]{1,0:T(8,128)S(1)}, u32[]{:S(2)}, u32[]{:S(2)}) collective-permute-start(f32[1024,512]{1,0:T(8,128)S(1)} %fusion), channel_id=1, source_target_pairs={{8,0},{16,8},{24,16},{9,1},{17,9},{25,17},{10,2},{18,10},{26,18},{... | collective-permute-start | bytes 6291464 | tf_op jit(solution)/shard_map/ppermute | solution.py:201
  271.2 9.2 %collective-permute-start.12 = (f32[1024,512]{1,0:T(8,128)S(1)}, f32[1024,512]{1,0:T(8,128)S(1)}, u32[]{:S(2)}, u32[]{:S(2)}) collective-permute-start(f32[1024,512]{1,0:T(8,128)S(1)} %collective-permute-done.11), channel_id=1, source_target_pairs={{8,16},{16,24},{9,17},{17,25},{10,18},{18,26},{11,19},{19,27},{12,... | collective-permute-start | bytes 6291464 | tf_op jit(solution)/shard_map/ppermute | solution.py:200
  279.1 48.1 %collective-permute-start.14 = (f32[1024,512]{1,0:T(8,128)S(1)}, f32[1024,512]{1,0:T(8,128)S(1)}, u32[]{:S(2)}, u32[]{:S(2)}) collective-permute-start(f32[1024,512]{1,0:T(8,128)S(1)} %collective-permute-done.10), channel_id=1, source_target_pairs={{8,0},{16,8},{9,1},{17,9},{10,2},{18,10},{11,3},{19,11},{12,4},{20... | collective-permute-start | bytes 6291464 | tf_op jit(solution)/shard_map/ppermute | solution.py:201
  280.4 62.0 %collective-permute-start.13 = (f32[1024,512]{1,0:T(8,128)S(1)}, f32[1024,512]{1,0:T(8,128)S(1)}, u32[]{:S(2)}, u32[]{:S(2)}) collective-permute-start(f32[1024,512]{1,0:T(8,128)S(1)} %collective-permute-done.12), channel_id=1, source_target_pairs={{16,24},{17,25},{18,26},{19,27},{20,28},{21,29},{22,30},{23,31}} | collective-permute-start | bytes 6291464 | tf_op jit(solution)/shard_map/ppermute | solution.py:200
  327.2 46.7 %collective-permute-start.15 = (f32[1024,512]{1,0:T(8,128)S(1)}, f32[1024,512]{1,0:T(8,128)S(1)}, u32[]{:S(2)}, u32[]{:S(2)}) collective-permute-start(f32[1024,512]{1,0:T(8,128)S(1)} %collective-permute-done.14), channel_id=1, source_target_pairs={{8,0},{9,1},{10,2},{11,3},{12,4},{13,5},{14,6},{15,7}} | collective-permute-start | bytes 6291464 | tf_op jit(solution)/shard_map/ppermute | solution.py:201
  380.1 11.2 %collective-permute-start.17 = (f32[1,8,512]{2,1,0:T(8,128)}, f32[1,8,512]{2,1,0:T(8,128)S(1)}, u32[]{:S(2)}, u32[]{:S(2)}) collective-permute-start(f32[1,8,512]{2,1,0:T(8,128)} %get-tuple-element.23), channel_id=1, source_target_pairs={{8,0},{16,8},{24,16},{9,1},{17,9},{25,17},{10,2},{18,10},{26,18},{... | collective-permute-start | bytes 49160 | tf_op jit(solution)/shard_map/ppermute | solution.py:40
  382.6 12.2 %collective-permute-start.16 = (f32[1,8,512]{2,1,0:T(8,128)}, f32[1,8,512]{2,1,0:T(8,128)}, u32[]{:S(2)}, u32[]{:S(2)}) collective-permute-start(f32[1,8,512]{2,1,0:T(8,128)} %get-tuple-element.24), channel_id=1, source_target_pairs={{0,8},{8,16},{16,24},{1,9},{9,17},{17,25},{2,10},{10,18},{18,26},{... | collective-permute-start | bytes 49160 | tf_op jit(solution)/shard_map/ppermute | solution.py:39
  391.4 33.5 %copy-start.7 = (f32[1,8,512]{2,1,0:T(8,128)}, f32[1,8,512]{2,1,0:T(8,128)S(1)}, u32[]{:S(2)}) copy-start(f32[1,8,512]{2,1,0:T(8,128)S(1)} %collective-permute-done.17.refs_4_) | copy-start | bytes 49156
  400.2 52.9 %collective-permute-start.19 = (f32[1,1040,2]{1,2,0:T(2,128)}, f32[1,1040,2]{1,2,0:T(2,128)}, u32[]{:S(2)}, u32[]{:S(2)}) collective-permute-start(f32[1,1040,2]{1,2,0:T(2,128)} %concatenate.31), channel_id=1, source_target_pairs={{1,0},{2,1},{3,2},{4,3},{5,4},{6,5},{7,6},{9,8},{10,9},{11,10},{12... | collective-permute-start | bytes 24968 | tf_op jit(solution)/shard_map/ppermute | solution.py:49
  402.9 50.2 %collective-permute-start.18 = (f32[1,1040,2]{1,2,0:T(2,128)}, f32[1,1040,2]{1,2,0:T(2,128)}, u32[]{:S(2)}, u32[]{:S(2)}) collective-permute-start(f32[1,1040,2]{1,2,0:T(2,128)} %concatenate.30), channel_id=1, source_target_pairs={{0,1},{1,2},{2,3},{3,4},{4,5},{5,6},{6,7},{8,9},{9,10},{10,11},{11... | collective-permute-start | bytes 24968 | tf_op jit(solution)/shard_map/ppermute | solution.py:48
  425.5 12.6 %collective-permute-start.21 = (f32[1,8,512]{2,1,0:T(8,128)}, f32[1,8,512]{2,1,0:T(8,128)S(1)}, u32[]{:S(2)}, u32[]{:S(2)}) collective-permute-start(f32[1,8,512]{2,1,0:T(8,128)} %get-tuple-element.19), channel_id=1, source_target_pairs={{8,0},{16,8},{24,16},{9,1},{17,9},{25,17},{10,2},{18,10},{26,18},{... | collective-permute-start | bytes 49160 | tf_op jit(solution)/shard_map/ppermute | solution.py:40
  429.3 9.4 %collective-permute-start.20 = (f32[1,8,512]{2,1,0:T(8,128)}, f32[1,8,512]{2,1,0:T(8,128)}, u32[]{:S(2)}, u32[]{:S(2)}) collective-permute-start(f32[1,8,512]{2,1,0:T(8,128)} %get-tuple-element.20), channel_id=1, source_target_pairs={{0,8},{8,16},{16,24},{1,9},{9,17},{17,25},{2,10},{10,18},{18,26},{... | collective-permute-start | bytes 49160 | tf_op jit(solution)/shard_map/ppermute | solution.py:39
  446.8 11.3 %collective-permute-start.23 = (f32[1,1040,2]{1,2,0:T(2,128)}, f32[1,1040,2]{1,2,0:T(2,128)}, u32[]{:S(2)}, u32[]{:S(2)}) collective-permute-start(f32[1,1040,2]{1,2,0:T(2,128)} %concatenate.34), channel_id=1, source_target_pairs={{1,0},{2,1},{3,2},{4,3},{5,4},{6,5},{7,6},{9,8},{10,9},{11,10},{12... | collective-permute-start | bytes 24968 | tf_op jit(solution)/shard_map/ppermute | solution.py:49
  449.5 8.6 %collective-permute-start.22 = (f32[1,1040,2]{1,2,0:T(2,128)}, f32[1,1040,2]{1,2,0:T(2,128)}, u32[]{:S(2)}, u32[]{:S(2)}) collective-permute-start(f32[1,1040,2]{1,2,0:T(2,128)} %concatenate.33), channel_id=1, source_target_pairs={{0,1},{1,2},{2,3},{3,4},{4,5},{5,6},{6,7},{8,9},{9,10},{10,11},{11... | collective-permute-start | bytes 24968 | tf_op jit(solution)/shard_map/ppermute | solution.py:48
  464.8 13.4 %copy-start.8 = (f32[1,8,512]{2,1,0:T(8,128)S(1)}, f32[1,8,512]{2,1,0:T(8,128)}, u32[]{:S(2)}) copy-start(f32[1,8,512]{2,1,0:T(8,128)} %copy-done.7) | copy-start | bytes 49156
  (8 other events, 33.8 us)
Sparse Core Ops, SparseCore 0:
  56.0 93.1 all-gather.5
  225.5 92.6 all-gather.3
